TPU v7x, 32 devices: a whole 2x2x4 slice. The times are simulated.
32 devices in a mesh: seq: 8 (over y, x, core), head: 2 (over z_hi), var: 2 (over z_lo).
Axes of the slice: x: 2, y: 2, z: 4 (z_hi: 2, z_lo: 2; z = z_hi * 2 + z_lo), core: 2. Of those that a mesh axis runs over, the one named last changes fastest.
Arguments:
- inner: bfloat16 [512, 1024], P('seq', 'head'), may hold values from -4.5 to 4.5
- residual_in: bfloat16 [512, 4096], P('seq', 'head'), may hold values from -6 to 6
- erase: int32 [2, 512], P('var', 'seq'), parts along dimension 0, may hold values from 0 to 1, as said below
- conv_weight: float32 [4, 1024], P(None, 'head'), may hold values from -3 to 3
- qkv_weight: bfloat16 [2, 512, 1536], P('head'), may hold values from -0.25 to 0.25
- gate_weight: bfloat16 [2, 2, 512], P('head'), may hold values from -0.4075734 to 0.4075734, as said below
- gate_bias: float32 [2, 2], P('head'), as said below
- norm_gain: float32 [1024], P('head'), may hold values from 0.5 to 1.5
- down_weight: bfloat16 [1024, 4096], P('head', 'seq'), may hold values from -0.1875 to 0.1875
Outputs:
- mixed: bfloat16 [2, 512, 4096], P('var', 'seq', 'head'), parts along dimension 0
There are 2 independent parts, one for each index of `var`. A program takes and returns all parts, laid end to end along the dimension named above; an argument that names none is the same for every part. Nothing has to cross between parts.
Inputs may be any that keep to these rules, and one draw needn't show every extreme that they name: `erase`: each variant erases a few runs of consecutive tokens. `gate_weight`: row 0 of each head holds the input gate projection and row 1 the forget gate projection. `gate_bias`: column 0 is the input gate bias and column 1 the forget gate bias of each head.
All inputs are finite; a program needn't handle non-finite values.
Results may differ from a plain program's by a relative error of at most 0.014.
Values may be sent and summed in bfloat16 or wider, within the bound.
A program may use at most 128 MiB of HBM per device.

v0:
```python
import jax
import jax.numpy as jnp
from jax import lax
from jax.sharding import PartitionSpec as P

CONV = 4


def carried_in(value, axis, join, neutral):
    count, mine = (lax.axis_size(axis), lax.axis_index(axis))
    pieces = jax.tree.map(lambda part: lax.all_gather(part, axis), value)
    subtotal = jax.tree.map(
        lambda part, zero: jnp.full_like(part, 0) + jnp.asarray(zero, part.dtype), value, neutral
    )

    def hop(position, subtotal):
        longer = join(subtotal, jax.tree.map(lambda part: part[position], pieces))
        return jax.tree.map(lambda new, old: jnp.where(position < mine, new, old), longer, subtotal)

    return lax.fori_loop(0, count - 1, hop, subtotal)


def from_behind(value, axis, steps):
    count = lax.axis_size(axis)
    initial, last = (max(0, -steps), min(count, count - steps))
    return lax.ppermute(value, axis, [(source, source + steps) for source in range(initial, last)])


def combine_states(earlier, later):
    return (earlier[0] + later[0], jnp.exp(later[0])[:, None, None] * earlier[1] + later[1])


def entering_state(block_decay, own_memory):
    identity = (jnp.zeros_like(block_decay), jnp.zeros_like(own_memory))
    return carried_in((block_decay, own_memory), "seq", combine_states, identity)


def local_terms(queries, key_rows, values, cumulated, input_log):
    token_count = queries.shape[1]
    causal = jnp.arange(token_count)[:, None] >= jnp.arange(token_count)[None, :]
    scores = jnp.einsum("vtd,vsd->vts", queries, key_rows, preferred_element_type=jnp.float32)
    exponent = cumulated[:, :, None] - cumulated[:, None, :] + input_log[:, None, :]
    weights = (scores * jnp.exp(jnp.where(causal, exponent, -jnp.inf))).astype(jnp.bfloat16)
    return jnp.einsum("vts,vse->vte", weights, values, preferred_element_type=jnp.float32)


def body(
    inner,
    residual_in,
    erase,
    conv_weight,
    qkv_weight,
    gate_weight,
    gate_bias,
    norm_gain,
    down_weight,
):
    columns_all = lax.all_gather(down_weight, "seq", axis=1, tiled=True)
    kept_mask = (1 - erase).astype(jnp.bfloat16)
    erased = inner[None, :, :] * kept_mask[:, :, None]
    row_count = inner.shape[0]
    last_rows = erased[:, row_count - (CONV - 1) :, :]
    prior_rows = from_behind(last_rows, "seq", 1)
    window = jnp.concatenate([prior_rows, erased], axis=1).astype(jnp.float32)
    convolved = jnp.zeros(erased.shape, jnp.float32)
    for offset in range(CONV):
        convolved = (
            convolved
            + conv_weight[offset] * window[:, CONV - 1 - offset : CONV - 1 - offset + row_count]
        )
    activated = jax.nn.silu(convolved).astype(jnp.bfloat16)
    proj_head = qkv_weight[0]
    head_size = proj_head.shape[0]
    query_key = jnp.einsum(
        "vtd,de->vte", activated, proj_head[:, : 2 * head_size], preferred_element_type=jnp.float32
    )
    queries = query_key[..., :head_size].astype(jnp.bfloat16)
    key_rows = (query_key[..., head_size:] * head_size ** (-0.5)).astype(jnp.bfloat16)
    values = jnp.einsum(
        "vtd,de->vte", erased, proj_head[:, 2 * head_size :], preferred_element_type=jnp.float32
    ).astype(jnp.bfloat16)
    gate_pre = (
        jnp.einsum("vtd,gd->vtg", activated, gate_weight[0], preferred_element_type=jnp.float32)
        + gate_bias[0]
    )
    input_log = 15.0 * jnp.tanh(gate_pre[..., 0] / 15.0)
    forget_log = jax.nn.log_sigmoid(gate_pre[..., 1])
    cumulated = jnp.cumsum(forget_log, axis=1)
    block_decay = cumulated[:, -1]
    key_scale = jnp.exp(block_decay[:, None] - cumulated + input_log)
    scaled_keys = (key_scale[..., None] * key_rows.astype(jnp.float32)).astype(jnp.bfloat16)
    own_memory = jnp.einsum("vsd,vse->vde", scaled_keys, values, preferred_element_type=jnp.float32)
    prior_decay, memory = entering_state(block_decay, own_memory)
    intra_part = local_terms(queries, key_rows, values, cumulated, input_log)
    memory_rounded = memory.astype(jnp.bfloat16)
    carry_part = jnp.einsum(
        "vtd,vde->vte", queries, memory_rounded, preferred_element_type=jnp.float32
    )
    numerator = jnp.exp(cumulated)[..., None] * carry_part + intra_part
    row_mean = jnp.mean(numerator, axis=-1, keepdims=True)
    centred = numerator - row_mean
    row_var = jnp.mean(centred * centred, axis=-1, keepdims=True)
    normed = (centred * lax.rsqrt(row_var + 1e-05) * norm_gain).astype(jnp.bfloat16)
    head_terms = (
        jnp.einsum("vtd,dc->vtc", normed, columns_all, preferred_element_type=jnp.float32)
        .astype(jnp.bfloat16)
        .astype(jnp.float32)
    )
    summed = lax.psum_scatter(
        head_terms.astype(jnp.bfloat16), "head", scatter_dimension=2, tiled=True
    ).astype(jnp.float32)
    return (residual_in[None, :, :].astype(jnp.float32) + summed).astype(jnp.bfloat16)


def solution(mesh):
    in_specs = (
        P("seq", "head"),
        P("seq", "head"),
        P("var", "seq"),
        P(None, "head"),
        P("head", None, None),
        P("head", None, None),
        P("head", None),
        P("head"),
        P("head", "seq"),
    )
    out_specs = P("var", "seq", "head")
    return jax.shard_map(body, mesh=mesh, in_specs=in_specs, out_specs=out_specs, check_vma=False)
```

profile of v0, /device:TPU:0, one launch (start us, length us, event | category | flops | bytes accessed | tf_op | source)
XLA Modules:
  0.0 148.6 jit_solution(74866529121974130)
XLA Ops:
  6.5 0.7 convert_bitcast_fusion
  7.2 0.9 multiply_bitcast_fusion
  8.2 2.4 %collective-permute-start = (bf16[1,3,512]{2,1,0:T(4,128)(2,1)S(1)}, bf16[1,3,512]{2,1,0:T(4,128)(2,1)S(1)}, u32[]{:S(2)}, u32[]{:S(2)}) collective-permute-start(bf16[1,3,512]{2,1,0:T(4,128)(2,1)S(1)} %slice.65), channel_id=1, source_target_pairs={{0,4},{4,8},{8,12},{12,16},{16,20},{20,24},{24,28},{1,5},{5,9},{9,... | collective-permute-start | bytes 9224 | tf_op jit(solution)/shard_map/ppermute | solution.py:26
  10.5 1.3 convolution_convert_fusion.1
  11.9 0.9 fusion.57
  12.9 1.5 %convolution_bitcast_fusion = f32[1,64,1024]{2,1,0:T(8,128)S(1)} fusion(bf16[512,1536]{1,0:T(8,128)(2,1)} %bitcast.96, bf16[1,64,512]{2,1,0:T(8,128)(2,1)S(1)} %multiply_convert_fusion.2), kind=kOutput, calls=%fused_computation.5 | convolution fusion | flops 67108864 | bytes 1376256 | tf_op jit(solution)/shard_map/vtd,de->vte/dot_general | solution.py:74
  14.4 0.7 fusion.5
  16.0 0.7 fusion.46
  16.7 1.4 fusion.16
  18.2 0.7 all-gather.4.cloned.1.call-update
  19.0 0.6 dynamic-slice
  19.6 1.3 bitcast_dynamic-update-slice_fusion
  21.0 14.6 %all-reduce = f32[8]{0:T(128)S(1)} all-reduce(f32[8]{0:T(128)S(1)} %bitcast_dynamic-update-slice_fusion), channel_id=1, replica_groups=mesh['seq'=8,'head'=2,'var'=2] {'seq'}, use_global_device_ids=true, to_apply=%add | all-reduce | flops 8 | bytes 64
  35.9 39.9 %all-gather.6.cloned.1.call-done = f32[4096,512]{1,0:T(8,128)} async-done(((f32[512,512]{1,0:T(8,128)}), f32[4096,512]{1,0:T(8,128)}) %all-gather.6.cloned.1.call-update) | async-done | bytes 8388624 | tf_op jit(solution)/shard_map/all_gather | solution.py:11
  75.8 21.3 %while.14 = (s32[]{:T(128)}, f32[1,512,512]{2,1,0:T(8,128)S(1)}, s32[]{:T(128)}, f32[8,1]{0,1:T(1,128)S(1)}, f32[8,1,512,512]{3,2,1,0:T(8,128)}, /*index=5*/s32[]{:T(128)}, s32[]{:T(128)}) while((s32[]{:T(128)}, f32[1,512,512]{2,1,0:T(8,128)S(1)}, s32[]{:T(128)}, f32[8,1]{0,1:T(1,128)S(1)}, f32[8,1,512,512]{3,2,1,0:T(8,128)}, ...), condition=%wide.region_2.3_spmd.clone, body=%wide.region_1.2_spmd.clone.sunk | while | flops 1048580 | bytes 3145845 | solution.py:20
  76.4 2.4 %fusion.65 = f32[1,512,512]{2,1,0:T(8,128)S(1)} fusion(f32[8,1,512,512]{3,2,1,0:T(8,128)} %get-tuple-element.190, s32[]{:T(128)} %get-tuple-element.179, f32[1,512,512]{2,1,0:T(8,128)S(1)} %get-tuple-element.180, f32[]{:T(128)} %bitcast.93, pred[]{:T(512)S(6)} %compare.3, pred[]{:T(512)S(6)} %lt.22), kind=kLoop, calls=%fused_computation.1.clone.1 | loop fusion | flops 1048576 | bytes 3145738 | tf_op jit(solution)/shard_map/while/body/eval_jaxpr/jit(_where)/select_n | solution.py:18
  78.8 0.6 fusion.64
  79.4 2.4 %fusion.65 = f32[1,512,512]{2,1,0:T(8,128)S(1)} fusion(f32[8,1,512,512]{3,2,1,0:T(8,128)} %get-tuple-element.190, s32[]{:T(128)} %get-tuple-element.179, f32[1,512,512]{2,1,0:T(8,128)S(1)} %get-tuple-element.180, f32[]{:T(128)} %bitcast.93, pred[]{:T(512)S(6)} %compare.3, pred[]{:T(512)S(6)} %lt.22), kind=kLoop, calls=%fused_computation.1.clone.1 | loop fusion | flops 1048576 | bytes 3145738 | tf_op jit(solution)/shard_map/while/body/eval_jaxpr/jit(_where)/select_n | solution.py:18
  81.8 0.6 fusion.64
  82.5 2.5 %fusion.65 = f32[1,512,512]{2,1,0:T(8,128)S(1)} fusion(f32[8,1,512,512]{3,2,1,0:T(8,128)} %get-tuple-element.190, s32[]{:T(128)} %get-tuple-element.179, f32[1,512,512]{2,1,0:T(8,128)S(1)} %get-tuple-element.180, f32[]{:T(128)} %bitcast.93, pred[]{:T(512)S(6)} %compare.3, pred[]{:T(512)S(6)} %lt.22), kind=kLoop, calls=%fused_computation.1.clone.1 | loop fusion | flops 1048576 | bytes 3145738 | tf_op jit(solution)/shard_map/while/body/eval_jaxpr/jit(_where)/select_n | solution.py:18
  84.9 0.6 fusion.64
  85.6 2.4 %fusion.65 = f32[1,512,512]{2,1,0:T(8,128)S(1)} fusion(f32[8,1,512,512]{3,2,1,0:T(8,128)} %get-tuple-element.190, s32[]{:T(128)} %get-tuple-element.179, f32[1,512,512]{2,1,0:T(8,128)S(1)} %get-tuple-element.180, f32[]{:T(128)} %bitcast.93, pred[]{:T(512)S(6)} %compare.3, pred[]{:T(512)S(6)} %lt.22), kind=kLoop, calls=%fused_computation.1.clone.1 | loop fusion | flops 1048576 | bytes 3145738 | tf_op jit(solution)/shard_map/while/body/eval_jaxpr/jit(_where)/select_n | solution.py:18
  88.0 0.6 fusion.64
  88.6 2.4 %fusion.65 = f32[1,512,512]{2,1,0:T(8,128)S(1)} fusion(f32[8,1,512,512]{3,2,1,0:T(8,128)} %get-tuple-element.190, s32[]{:T(128)} %get-tuple-element.179, f32[1,512,512]{2,1,0:T(8,128)S(1)} %get-tuple-element.180, f32[]{:T(128)} %bitcast.93, pred[]{:T(512)S(6)} %compare.3, pred[]{:T(512)S(6)} %lt.22), kind=kLoop, calls=%fused_computation.1.clone.1 | loop fusion | flops 1048576 | bytes 3145738 | tf_op jit(solution)/shard_map/while/body/eval_jaxpr/jit(_where)/select_n | solution.py:18
  91.0 0.6 fusion.64
  91.7 2.4 %fusion.65 = f32[1,512,512]{2,1,0:T(8,128)S(1)} fusion(f32[8,1,512,512]{3,2,1,0:T(8,128)} %get-tuple-element.190, s32[]{:T(128)} %get-tuple-element.179, f32[1,512,512]{2,1,0:T(8,128)S(1)} %get-tuple-element.180, f32[]{:T(128)} %bitcast.93, pred[]{:T(512)S(6)} %compare.3, pred[]{:T(512)S(6)} %lt.22), kind=kLoop, calls=%fused_computation.1.clone.1 | loop fusion | flops 1048576 | bytes 3145738 | tf_op jit(solution)/shard_map/while/body/eval_jaxpr/jit(_where)/select_n | solution.py:18
  94.1 0.6 fusion.64
  94.7 2.4 %fusion.65 = f32[1,512,512]{2,1,0:T(8,128)S(1)} fusion(f32[8,1,512,512]{3,2,1,0:T(8,128)} %get-tuple-element.190, s32[]{:T(128)} %get-tuple-element.179, f32[1,512,512]{2,1,0:T(8,128)S(1)} %get-tuple-element.180, f32[]{:T(128)} %bitcast.93, pred[]{:T(512)S(6)} %compare.3, pred[]{:T(512)S(6)} %lt.22), kind=kLoop, calls=%fused_computation.1.clone.1 | loop fusion | flops 1048576 | bytes 3145738 | tf_op jit(solution)/shard_map/while/body/eval_jaxpr/jit(_where)/select_n | solution.py:18
  97.6 17.5 %all-gather.4.cloned.1.call-done = bf16[512,4096]{1,0:T(8,128)(2,1)} async-done(((bf16[512,512]{1,0:T(8,128)(2,1)}), bf16[512,4096]{1,0:T(8,128)(2,1)}) %all-gather.4.cloned.1.call-update) | async-done | bytes 4194320 | tf_op jit(solution)/shard_map/all_gather | solution.py:58
  115.1 3.9 %fusion.1 = bf16[1,64,4096]{2,1,0:T(8,128)(2,1)} fusion(bf16[512,4096]{1,0:T(8,128)(2,1)} %all-gather.4.cloned.1.call-done, f32[64,512]{1,0:T(8,128)S(1)} %get-tuple-element.140, f32[512]{0:T(512)S(1)} %copy-done.2, f32[64]{0:T(128)S(1)} %add_rsqrt_fusion, f32[64]{0:T(128)S(1)} %broadcast_multiply_fusion), kind=kOutput, calls=%fused_computation.4 | convolution fusion | flops 268828672 | bytes 4852224 | tf_op jit(solution)/shard_map/vtd,dc->vtc/dot_general | solution.py:105
  119.0 21.3 %reduce-scatter.2.cloned.1.call-done = bf16[1,64,2048]{2,1,0:T(8,128)(2,1)} async-done(((bf16[1,64,4096]{2,1,0:T(8,128)(2,1)}), bf16[1,64,2048]{2,1,0:T(8,128)(2,1)}) %reduce-scatter.2.cloned.1.call-update) | async-done | bytes 262160 | tf_op jit(solution)/shard_map/reduce_scatter | solution.py:109
  140.3 1.7 %fusion.8 = bf16[1,64,2048]{2,1,0:T(8,128)(2,1)} fusion(bf16[1,64,2048]{2,1,0:T(8,128)(2,1)} %reduce-scatter.2.cloned.1.call-done, bf16[64,2048]{1,0:T(8,128)(2,1)S(1)} %copy-done.1), kind=kLoop, calls=%fused_computation.17 | loop fusion | flops 524288 | bytes 786432 | tf_op jit(solution)/shard_map/convert_element_type | solution.py:112
  (29 shorter events, 2.6 us)
Async XLA Ops:
  6.5 7.8 %copy-start = (bf16[1,2,512]{2,1,0:T(2,128)(2,1)S(1)}, bf16[1,2,512]{2,1,0:T(2,128)(2,1)}, u32[]{:S(2)}) copy-start(bf16[1,2,512]{2,1,0:T(2,128)(2,1)} %param.16) | copy-start | bytes 6148
  6.5 12.4 %copy-start.3 = (u32[32]{0:T(128)S(1)}, u32[32]{0:T(128)}, u32[]{:S(2)}) copy-start(u32[32]{0:T(128)} %constant.64) | copy-start | bytes 388
  6.5 69.3 %all-gather.6.cloned.1.call-start = ((), (), s32[]{:S(2)}) async-start(), calls=%async_computation.3 | async-start | bytes 9437184 | tf_op jit(solution)/shard_map/all_gather | solution.py:11
  8.2 4.6 %collective-permute-start = (bf16[1,3,512]{2,1,0:T(4,128)(2,1)S(1)}, bf16[1,3,512]{2,1,0:T(4,128)(2,1)S(1)}, u32[]{:S(2)}, u32[]{:S(2)}) collective-permute-start(bf16[1,3,512]{2,1,0:T(4,128)(2,1)S(1)} %slice.65), channel_id=1, source_target_pairs={{0,4},{4,8},{8,12},{12,16},{16,20},{20,24},{24,28},{1,5},{5,9},{9,... | collective-permute-start | bytes 9224 | tf_op jit(solution)/shard_map/ppermute | solution.py:26
  18.1 97.0 %all-gather.4.cloned.1.call-start = ((), (), s32[]{:S(2)}) async-start(), calls=%async_computation.1 | async-start | bytes 4718592 | tf_op jit(solution)/shard_map/all_gather | solution.py:58
  18.9 121.4 %reduce-scatter.2.cloned.1.call-start = ((), (), s32[]{:S(2)}) async-start(), calls=%async_computation.2 | async-start | bytes 786432 | tf_op jit(solution)/shard_map/reduce_scatter | solution.py:109
  75.8 39.3 %copy-start.2 = (f32[512]{0:T(512)S(1)}, f32[512]{0:T(512)}, u32[]{:S(2)}) copy-start(f32[512]{0:T(512)} %param.18) | copy-start | bytes 6148
  97.1 43.2 %copy-start.1 = (bf16[64,2048]{1,0:T(8,128)(2,1)S(1)}, bf16[64,2048]{1,0:T(8,128)(2,1)}, u32[]{:S(2)}) copy-start(bf16[64,2048]{1,0:T(8,128)(2,1)} %param.12) | copy-start | bytes 786436
Sparse Core Ops, SparseCore 0:
  18.3 57.4 all-gather.5
  77.7 37.4 all-gather.3
  119.2 21.0 reduce-scatter.1
where the time goes:
time: 149 us
  waiting for transfers between devices  79.4 us (53%)
  other arithmetic  21.4 us (14%)
  blocking collectives  14.6 us (10%)
  between operations  13.2 us (9%)
  matrix products  9.49 us (6%)
  local copies, waits for them, and re-layouts  7.85 us (5%)
  starting transfers between devices  2.44 us (2%)
    all_gather x1, waiting for transfers between devices, carried_in(): pieces = jax.tree.map(lambda part: lax.all_gather(part, axis), value)  39.9 us
    reduce_scatter x1, waiting for transfers between devices, body(): lax.psum_scatter(head_terms.astype(jnp.bfloat16), 'head', scatter_dimensi...  21.3 us
    all_gather x1, waiting for transfers between devices, body(): columns_all = lax.all_gather(down_weight, 'seq', axis=1, tiled=True)  17.5 us
    select_n x7, other arithmetic, hop(): jnp.where(position < mine, new, old)  16.8 us
    unnamed x1, blocking collectives  14.6 us
    exp x7, local copies, waits for them, and re-layouts, combine_states(): jnp.exp(later[0])[:, None, None] * earlier[1] + later[1]  4.37 us
    dot_general x1, matrix products, body(): jnp.einsum('vtd,dc->vtc', normed, columns_all, preferred_element_type=jnp...  3.87 us
  transfers between devices with their start and end apart: 4, of which 3 were waited for; matrix products, arithmetic and copies ran while one was open for 18% of the time, Pallas kernels for 0%

commit v1 on v0

v1 whole, which is shorter than its diff:
```python
import functools

import jax
import jax.numpy as jnp
from jax import lax
from jax.experimental import pallas as pl
from jax.experimental.pallas import tpu as pltpu
from jax.sharding import PartitionSpec as P

CONV = 4
PAD = 16
GROUP = 4
MESH = pl.DeviceIdType.MESH
BF16 = jnp.bfloat16
F32 = jnp.float32


def dot_nt(a, b):
    return lax.dot_general(a, b, (((1,), (1,)), ((), ())), preferred_element_type=F32)


def dot_nn(a, b):
    return jnp.dot(a, b, preferred_element_type=F32)


def as_column(row, eye):
    return jnp.sum(jnp.where(eye, row, 0.0), axis=1, keepdims=True)


def kernel(
    n_seq,
    n_head,
    inner_ref,
    erase_ref,
    conv_ref,
    gate_ref,
    bias_ref,
    gain_ref,
    proj_hbm,
    down_hbm,
    resid_hbm,
    out_ref,
    rows,
    proj,
    down,
    resid,
    keys,
    vals,
    tails,
    part,
    landed,
    load_sem,
    row_send,
    row_recv,
    part_send,
    part_recv,
    self_sem,
):
    seq, head = lax.axis_index("seq"), lax.axis_index("head")
    tok, width = inner_ref.shape
    columns = down.shape[1]
    per_head = n_seq // n_head
    chunk = GROUP * tok
    chunks = n_seq // GROUP
    small = chunks <= 2
    out_head, out_slot = seq // per_head, lax.rem(seq, per_head)

    def loop(count, step, carry=None):
        if small:
            for position in range(count):
                carry = step(position, carry)
            return carry
        return lax.fori_loop(0, count, step, carry)

    barrier = pltpu.get_barrier_semaphore()
    group = n_seq * n_head
    flat = seq * n_head + head

    def greet(step, carry):
        other = lax.rem(flat + step + 1, group)
        pl.semaphore_signal(
            barrier,
            inc=1,
            device_id={"seq": other // n_head, "head": lax.rem(other, n_head)},
            device_id_type=MESH,
        )
        return carry

    loop(group - 1, greet, 0)

    loads = [
        pltpu.make_async_copy(proj_hbm.at[0], proj, load_sem.at[0]),
        pltpu.make_async_copy(down_hbm, down, load_sem.at[1]),
        pltpu.make_async_copy(resid_hbm, resid, load_sem.at[2]),
    ]
    for load in loads:
        load.start()

    rows[pl.ds(0, PAD), :] = jnp.zeros((PAD, width), BF16)
    line = lax.broadcasted_iota(jnp.int32, (tok, tok), 0)
    lane = lax.broadcasted_iota(jnp.int32, (tok, tok), 1)
    kept = as_column((1 - erase_ref[...]).astype(F32), line == lane)
    own = pl.ds(pl.multiple_of(PAD + seq * tok, PAD), tok)
    rows[own, :] = (inner_ref[...].astype(F32) * kept).astype(BF16)

    pl.semaphore_wait(barrier, group - 1)

    def row_copy(block, target):
        place = pl.ds(pl.multiple_of(PAD + block * tok, PAD), tok)
        return pltpu.make_async_remote_copy(
            src_ref=rows.at[place],
            dst_ref=rows.at[place],
            send_sem=row_send.at[target],
            recv_sem=row_recv.at[block],
            device_id={"seq": target},
            device_id_type=MESH,
        )

    def send_rows(step, carry):
        row_copy(seq, lax.rem(seq + step + 1, n_seq)).start()
        return carry

    loop(n_seq - 1, send_rows, 0)

    line = lax.broadcasted_iota(jnp.int32, (chunk, chunk), 0)
    lane = lax.broadcasted_iota(jnp.int32, (chunk, chunk), 1)
    loads[0].wait()
    loads[1].wait()

    def part_copy(block, slot):
        return pltpu.make_async_remote_copy(
            src_ref=part.at[block],
            dst_ref=landed.at[head, out_slot],
            send_sem=part_send.at[block],
            recv_sem=part_recv.at[head, out_slot],
            device_id={"seq": block, "head": out_head},
            device_id_type=MESH,
        )

    def work(index, carry):
        start = index * chunk if small else pl.multiple_of(index * chunk, chunk)
        here = pl.ds(start, chunk)
        for position in range(GROUP):
            block = index * GROUP + position

            @pl.when(block != seq)
            def _():
                row_copy(block, lax.rem(seq + 1, n_seq)).wait_recv()

        window = rows[pl.ds(start, chunk + PAD), :].astype(F32)
        convolved = conv_ref[pl.ds(0, 1), :] * window[PAD:]
        for offset in range(1, CONV):
            convolved += conv_ref[pl.ds(offset, 1), :] * pltpu.roll(window, offset, 0)[PAD:]
        half = 0.5 * convolved
        activated = (half + half * jnp.tanh(half)).astype(BF16)
        erased = rows[pl.ds(start + PAD, chunk), :]
        gates = dot_nt(gate_ref[0], activated)
        input_log = 15.0 * jnp.tanh((gates[0:1] + bias_ref[0, 0]) / 15.0)
        forget = gates[1:2] + bias_ref[0, 1]
        forget_log = jnp.minimum(forget, 0.0) - jnp.log1p(jnp.exp(-jnp.abs(forget)))
        summed = jnp.dot(
            jnp.broadcast_to(forget_log, (8, chunk)),
            (line <= lane).astype(F32),
            preferred_element_type=F32,
            precision=lax.Precision.HIGHEST,
        )
        cumulated = summed[0:1]
        last = summed[0:1, chunk - 1 : chunk]
        by_row = as_column(cumulated, line == lane)
        queries = dot_nn(activated, proj[:, :width]).astype(BF16)
        key_rows = (dot_nn(activated, proj[:, width : 2 * width]) * width ** (-0.5)).astype(BF16)
        values = dot_nn(erased, proj[:, 2 * width :]).astype(BF16)
        keys[here, :] = key_rows
        vals[here, :] = values
        exponent = by_row + (input_log - cumulated)
        weights = dot_nt(queries, key_rows) * jnp.exp(jnp.where(line >= lane, exponent, -jnp.inf))
        numerator = dot_nn(weights.astype(BF16), values)

        def earlier(other, total):
            there = pl.ds(other * chunk if small else pl.multiple_of(other * chunk, chunk), chunk)
            tail = tails[other]
            scores = dot_nt(queries, keys[there, :])
            weights = (scores * jnp.exp(by_row + tail[0:1])).astype(BF16)
            tails[other] = tail + last
            return total + dot_nn(weights, vals[there, :])

        numerator = loop(index, earlier, numerator)
        tails[index] = jnp.broadcast_to(last - cumulated + input_log, (8, chunk))
        mean = jnp.mean(numerator, axis=1, keepdims=True)
        centred = numerator - mean
        variance = jnp.mean(centred * centred, axis=1, keepdims=True)
        normed = (centred * lax.rsqrt(variance + 1e-05) * gain_ref[...]).astype(BF16)
        product = dot_nn(normed, down[...]).astype(BF16)
        for position in range(GROUP):
            block = index * GROUP + position
            part[block] = product[position * tok : (position + 1) * tok]
            mine = (block == seq) & (out_head == head)

            @pl.when(jnp.logical_not(mine))
            def _():
                part_copy(block, 0).start()

            @pl.when(mine)
            def _():
                pltpu.make_async_copy(part.at[block], landed.at[head, out_slot], self_sem).start()

        return carry

    loop(chunks, work, 0)
    loads[2].wait()

    for slot in range(per_head):
        for other in range(n_head):
            source = head * per_head + slot
            mine = (source == seq) & (other == head)

            @pl.when(jnp.logical_not(mine))
            def _():
                pltpu.make_async_remote_copy(
                    src_ref=part.at[0],
                    dst_ref=landed.at[other, slot],
                    send_sem=part_send.at[0],
                    recv_sem=part_recv.at[other, slot],
                    device_id={"seq": lax.rem(seq + 1, n_seq)},
                    device_id_type=MESH,
                ).wait_recv()

            @pl.when(mine)
            def _():
                pltpu.make_async_copy(part.at[0], landed.at[head, out_slot], self_sem).wait()

        total = landed[0, slot].astype(F32)
        for other in range(1, n_head):
            total += landed[other, slot].astype(F32)
        place = pl.ds(slot * columns, columns)
        out_ref[0, :, place] = (resid[:, place].astype(F32) + total).astype(BF16)

    def sent_rows(step, carry):
        row_copy(seq, lax.rem(seq + step + 1, n_seq)).wait_send()
        return carry

    loop(n_seq - 1, sent_rows, 0)

    def sent_parts(block, carry):
        @pl.when(jnp.logical_not((block == seq) & (out_head == head)))
        def _():
            part_copy(block, 0).wait_send()

        return carry

    loop(n_seq, sent_parts, 0)


def body(
    n_seq,
    n_head,
    inner,
    residual_in,
    erase,
    conv_weight,
    qkv_weight,
    gate_weight,
    gate_bias,
    norm_gain,
    down_weight,
):
    tok, width = inner.shape
    columns = down_weight.shape[1]
    tokens = tok * n_seq
    chunk = GROUP * tok
    vmem = pl.BlockSpec(memory_space=pltpu.VMEM)
    anywhere = pl.BlockSpec(memory_space=pl.ANY)
    return pl.pallas_call(
        functools.partial(kernel, n_seq, n_head),
        out_shape=jax.ShapeDtypeStruct((1, tok, residual_in.shape[1]), BF16),
        in_specs=[vmem] * 4 + [pl.BlockSpec(memory_space=pltpu.SMEM), vmem] + [anywhere] * 3,
        out_specs=vmem,
        scratch_shapes=[
            pltpu.VMEM((PAD + tokens, width), BF16),
            pltpu.VMEM(qkv_weight.shape[1:], BF16),
            pltpu.VMEM(down_weight.shape, BF16),
            pltpu.VMEM(residual_in.shape, BF16),
            pltpu.VMEM((tokens, width), BF16),
            pltpu.VMEM((tokens, width), BF16),
            pltpu.VMEM((tokens // chunk, 8, chunk), F32),
            pltpu.VMEM((n_seq, tok, columns), BF16),
            pltpu.VMEM((n_head, n_seq // n_head, tok, columns), BF16),
            pltpu.SemaphoreType.DMA((3,)),
            pltpu.SemaphoreType.DMA((n_seq,)),
            pltpu.SemaphoreType.DMA((n_seq,)),
            pltpu.SemaphoreType.DMA((n_seq,)),
            pltpu.SemaphoreType.DMA((n_head, n_seq // n_head)),
            pltpu.SemaphoreType.DMA,
        ],
        compiler_params=pltpu.CompilerParams(
            collective_id=0, has_side_effects=True, vmem_limit_bytes=48 * 2**20
        ),
    )(
        inner,
        erase,
        conv_weight,
        gate_weight,
        gate_bias,
        norm_gain.reshape(1, width),
        qkv_weight,
        down_weight,
        residual_in,
    )


def solution(mesh):
    in_specs = (
        P("seq", "head"),
        P("seq", "head"),
        P("var", "seq"),
        P(None, "head"),
        P("head", None, None),
        P("head", None, None),
        P("head", None),
        P("head"),
        P("head", "seq"),
    )
    out_specs = P("var", "seq", "head")
    run = functools.partial(body, mesh.shape["seq"], mesh.shape["head"])
    return jax.shard_map(run, mesh=mesh, in_specs=in_specs, out_specs=out_specs, check_vma=False)
```

time: 149 us -> 47.6 us (0.32)
  the two profiles are of different devices: /device:TPU:0 before, /device:TPU:31 now
where the time goes in v1:
time: 47.6 us; the launch traced here: 46.9 us
  Pallas kernels  38.6 us (81%)
  local copies, waits for them, and re-layouts  8.31 us (17%)
    pallas_call x1, Pallas kernels, body(): pl.pallas_call(functools.partial(kernel, n_seq, n_head), out_shape=jax.Sh...  38.6 us
    unnamed x19, local copies, waits for them, and re-layouts  8.31 us

profile of v1, /device:TPU:31, one launch (start us, length us, event | category | flops | bytes accessed | tf_op | source)
XLA Modules:
  0.0 46.9 jit_solution(15636971123869206764)
XLA Ops:
  0.0 0.0 copy-start
  0.0 1.4 %copy-done = bf16[1,512,1536]{2,1,0:T(8,128)(2,1)S(1)} copy-done((bf16[1,512,1536]{2,1,0:T(8,128)(2,1)S(1)}, bf16[1,512,1536]{2,1,0:T(8,128)(2,1)}, u32[]{:S(2)}) %copy-start) | copy-done | bytes 1572888
  1.4 0.0 copy-start.1
  1.4 1.0 %copy-done.1 = bf16[512,512]{1,0:T(8,128)(2,1)S(1)} copy-done((bf16[512,512]{1,0:T(8,128)(2,1)S(1)}, bf16[512,512]{1,0:T(8,128)(2,1)}, u32[]{:S(2)}) %copy-start.1) | copy-done | bytes 524312
  2.5 0.0 copy-start.2
  2.5 0.9 %copy-done.2 = bf16[64,2048]{1,0:T(8,128)(2,1)S(1)} copy-done((bf16[64,2048]{1,0:T(8,128)(2,1)S(1)}, bf16[64,2048]{1,0:T(8,128)(2,1)}, u32[]{:S(2)}) %copy-start.2) | copy-done | bytes 262168
  3.4 0.0 copy-start.3
  3.4 0.8 %copy-done.3 = bf16[64,512]{1,0:T(8,128)(2,1)S(1)} copy-done((bf16[64,512]{1,0:T(8,128)(2,1)S(1)}, bf16[64,512]{1,0:T(8,128)(2,1)}, u32[]{:S(2)}) %copy-start.3) | copy-done | bytes 65560
  4.2 0.0 copy-start.4
  4.2 0.7 %copy-done.4 = f32[4,512]{1,0:T(4,128)S(1)} copy-done((f32[4,512]{1,0:T(4,128)S(1)}, f32[4,512]{1,0:T(4,128)}, u32[]{:S(2)}) %copy-start.4) | copy-done | bytes 8216
  4.9 0.0 copy-start.5
  4.9 0.7 %copy-done.5 = bf16[1,2,512]{2,1,0:T(2,128)(2,1)S(1)} copy-done((bf16[1,2,512]{2,1,0:T(2,128)(2,1)S(1)}, bf16[1,2,512]{2,1,0:T(2,128)(2,1)}, u32[]{:S(2)}) %copy-start.5) | copy-done | bytes 2072
  5.6 0.0 copy-start.6
  5.6 0.7 %copy-done.6 = f32[512]{0:T(512)S(1)} copy-done((f32[512]{0:T(512)S(1)}, f32[512]{0:T(512)}, u32[]{:S(2)}) %copy-start.6) | copy-done | bytes 2072
  6.3 0.0 copy-start.7
  6.3 0.7 %copy-done.7 = s32[1,64]{1,0:T(1,128)S(1)} copy-done((s32[1,64]{1,0:T(1,128)S(1)}, s32[1,64]{1,0:T(1,128)}, u32[]{:S(2)}) %copy-start.7) | copy-done | bytes 280
  7.0 0.0 copy-start.8
  7.0 0.7 %copy-done.8 = f32[1,2]{1,0:T(1,128)S(1)} copy-done((f32[1,2]{1,0:T(1,128)S(1)}, f32[1,2]{1,0:T(1,128)}, u32[]{:S(2)}) %copy-start.8) | copy-done | bytes 32
  7.6 38.6 %shard_map.91 = bf16[1,64,2048]{2,1,0:T(8,128)(2,1)S(1)} custom-call(bf16[64,512]{1,0:T(8,128)(2,1)S(1)} %copy-done.3, s32[1,64]{1,0:T(1,128)S(1)} %copy-done.7, f32[4,512]{1,0:T(4,128)S(1)} %copy-done.4, bf16[1,2,512]{2,1,0:T(2,128)(2,1)S(1)} %copy-done.5, f32[1,2]{1,0:T(1,128)S(1)} %copy-done.8, f32[1,512]{1,0:T(1,128)S(1)} %bitcast.1, ...), custom_call_target="tpu_custom_call" | custom-call | tf_op jit(solution)/shard_map/pallas_call | solution.py:273
  46.2 0.7 %copy.11 = bf16[1,64,2048]{2,1,0:T(8,128)(2,1)} copy(bf16[1,64,2048]{2,1,0:T(8,128)(2,1)S(1)} %shard_map.91) | data formatting | bytes 524288
Async XLA Ops:
  0.0 1.4 %copy-start = (bf16[1,512,1536]{2,1,0:T(8,128)(2,1)S(1)}, bf16[1,512,1536]{2,1,0:T(8,128)(2,1)}, u32[]{:S(2)}) copy-start(bf16[1,512,1536]{2,1,0:T(8,128)(2,1)} %proj_hbm.1) | copy-start | bytes 4718596
  1.4 1.0 %copy-start.1 = (bf16[512,512]{1,0:T(8,128)(2,1)S(1)}, bf16[512,512]{1,0:T(8,128)(2,1)}, u32[]{:S(2)}) copy-start(bf16[512,512]{1,0:T(8,128)(2,1)} %down_hbm.1) | copy-start | bytes 1572868
  2.5 0.9 %copy-start.2 = (bf16[64,2048]{1,0:T(8,128)(2,1)S(1)}, bf16[64,2048]{1,0:T(8,128)(2,1)}, u32[]{:S(2)}) copy-start(bf16[64,2048]{1,0:T(8,128)(2,1)} %resid_hbm.1) | copy-start | bytes 786436
  3.4 0.8 %copy-start.3 = (bf16[64,512]{1,0:T(8,128)(2,1)S(1)}, bf16[64,512]{1,0:T(8,128)(2,1)}, u32[]{:S(2)}) copy-start(bf16[64,512]{1,0:T(8,128)(2,1)} %inner_ref.1) | copy-start | bytes 196612
  4.2 0.7 %copy-start.4 = (f32[4,512]{1,0:T(4,128)S(1)}, f32[4,512]{1,0:T(4,128)}, u32[]{:S(2)}) copy-start(f32[4,512]{1,0:T(4,128)} %conv_ref.1) | copy-start | bytes 24580
  4.9 0.7 %copy-start.5 = (bf16[1,2,512]{2,1,0:T(2,128)(2,1)S(1)}, bf16[1,2,512]{2,1,0:T(2,128)(2,1)}, u32[]{:S(2)}) copy-start(bf16[1,2,512]{2,1,0:T(2,128)(2,1)} %gate_ref.1) | copy-start | bytes 6148
  5.6 0.7 %copy-start.6 = (f32[512]{0:T(512)S(1)}, f32[512]{0:T(512)}, u32[]{:S(2)}) copy-start(f32[512]{0:T(512)} %param.16) | copy-start | bytes 6148
  6.3 0.7 %copy-start.7 = (s32[1,64]{1,0:T(1,128)S(1)}, s32[1,64]{1,0:T(1,128)}, u32[]{:S(2)}) copy-start(s32[1,64]{1,0:T(1,128)} %erase_ref.1) | copy-start | bytes 772
  7.0 0.7 %copy-start.8 = (f32[1,2]{1,0:T(1,128)S(1)}, f32[1,2]{1,0:T(1,128)}, u32[]{:S(2)}) copy-start(f32[1,2]{1,0:T(1,128)} %bias_ref.1) | copy-start | bytes 28

commit v2 on v1

v2 whole, which is shorter than its diff:
```python
import functools

import jax
import jax.numpy as jnp
from jax import lax
from jax.experimental import pallas as pl
from jax.experimental.pallas import tpu as pltpu
from jax.sharding import PartitionSpec as P

CONV = 4
PAD = 16
GROUP = 4
MESH = pl.DeviceIdType.MESH
BF16 = jnp.bfloat16
F32 = jnp.float32


def dot_nt(a, b):
    return lax.dot_general(a, b, (((1,), (1,)), ((), ())), preferred_element_type=F32)


def dot_nn(a, b):
    return jnp.dot(a, b, preferred_element_type=F32)


def as_column(row, eye):
    return jnp.sum(jnp.where(eye, row, 0.0), axis=1, keepdims=True)


def kernel(
    n_seq,
    n_head,
    inner_hbm,
    erase_hbm,
    conv_hbm,
    gate_hbm,
    bias_ref,
    gain_hbm,
    proj_hbm,
    down_hbm,
    resid_hbm,
    out_ref,
    inner,
    erase,
    conv,
    gate,
    gain,
    proj,
    down,
    given,
    resid,
    rows,
    keys,
    vals,
    tails,
    part,
    landed,
    load_sem,
    row_send,
    row_recv,
    down_sem,
    part_send,
    part_recv,
    self_sem,
):
    seq, head = lax.axis_index("seq"), lax.axis_index("head")
    tok, width = inner.shape
    sides, _, piece = down.shape
    per_head = n_seq // n_head
    chunk = GROUP * tok
    chunks = n_seq // GROUP
    small = chunks <= 2
    out_head, out_slot = seq // per_head, lax.rem(seq, per_head)
    swap = sides == 2
    partner = lax.rem(seq + n_seq // 2, n_seq)
    sibling = seq + 1 - 2 * lax.rem(seq, 2)

    def loop(count, step, carry=None):
        if small:
            for position in range(count):
                carry = step(position, carry)
            return carry
        return lax.fori_loop(0, count, step, carry)

    loads = [
        pltpu.make_async_copy(source, target, load_sem.at[index])
        for index, (source, target) in enumerate(
            [
                (inner_hbm, inner),
                (erase_hbm, erase),
                (down_hbm.at[:, pl.ds((sides - 1) * piece, piece)], given if swap else down.at[0]),
                (proj_hbm.at[0], proj),
                (conv_hbm, conv),
                (gate_hbm.at[0], gate),
                (gain_hbm, gain),
                (resid_hbm, resid),
            ]
            + ([(down_hbm.at[:, pl.ds(0, piece)], down.at[0])] if swap else [])
        )
    ]
    for load in loads:
        load.start()

    barrier = pltpu.get_barrier_semaphore()
    group = n_seq * n_head
    flat = seq * n_head + head

    def greet(step, carry):
        other = lax.rem(flat + step + 1, group)
        pl.semaphore_signal(
            barrier,
            inc=1,
            device_id={"seq": other // n_head, "head": lax.rem(other, n_head)},
            device_id_type=MESH,
        )
        return carry

    loop(group - 1, greet, 0)

    rows[pl.ds(0, PAD), :] = jnp.zeros((PAD, width), BF16)
    line = lax.broadcasted_iota(jnp.int32, (tok, tok), 0)
    lane = lax.broadcasted_iota(jnp.int32, (tok, tok), 1)
    loads[0].wait()
    loads[1].wait()
    kept = as_column((1 - erase[...]).astype(F32), line == lane)
    own = pl.ds(pl.multiple_of(PAD + seq * tok, PAD), tok)
    rows[own, :] = (inner[...].astype(F32) * kept).astype(BF16)
    for load in loads[2:]:
        load.wait()

    pl.semaphore_wait(barrier, group - 1)

    def row_copy(block, target, slot):
        place = pl.ds(pl.multiple_of(PAD + block * tok, PAD), tok)
        return pltpu.make_async_remote_copy(
            src_ref=rows.at[place],
            dst_ref=rows.at[place],
            send_sem=row_send.at[slot],
            recv_sem=row_recv.at[block],
            device_id={"seq": target},
            device_id_type=MESH,
        )

    def send_rows(step, carry):
        row_copy(seq, lax.rem(seq + 2 * step + 2, n_seq), step).start()
        return carry

    loop(n_seq // 2 - 1, send_rows, 0)
    row_copy(seq, sibling, n_seq // 2 - 1).start()
    give = pltpu.make_async_remote_copy(
        src_ref=given if swap else down.at[0],
        dst_ref=down.at[sides - 1],
        send_sem=down_sem.at[0],
        recv_sem=down_sem.at[1],
        device_id={"seq": partner},
        device_id_type=MESH,
    )
    if swap:
        give.start()

    def forward(step, carry):
        block = lax.rem(seq + n_seq - 2 * step - 2, n_seq)
        row_copy(block, sibling, 0).wait_recv()
        row_copy(block, sibling, n_seq // 2 + step).start()
        return carry

    loop(n_seq // 2 - 1, forward, 0)

    line = lax.broadcasted_iota(jnp.int32, (chunk, chunk), 0)
    lane = lax.broadcasted_iota(jnp.int32, (chunk, chunk), 1)

    def part_copy(side, block, target):
        return pltpu.make_async_remote_copy(
            src_ref=part.at[side, block],
            dst_ref=landed.at[head, side, out_slot],
            send_sem=part_send.at[side, block],
            recv_sem=part_recv.at[head, side, out_slot],
            device_id={"seq": block, "head": target},
            device_id_type=MESH,
        )

    if swap:
        first = 1 - lax.rem(out_head + head, 2)
        routes = [(first, 1 - head), (1 - first, head)]
    else:
        routes = [(0, out_head)]

    def work(index, carry):
        start = index * chunk if small else pl.multiple_of(index * chunk, chunk)
        here = pl.ds(start, chunk)
        for position in range(GROUP):
            block = index * GROUP + position

            @pl.when(lax.rem(seq + block, 2) == 1)
            def _():
                row_copy(block, sibling, 0).wait_recv()

        window = rows[pl.ds(start, chunk + PAD), :].astype(F32)
        convolved = conv[pl.ds(0, 1), :] * window[PAD:]
        for offset in range(1, CONV):
            convolved += conv[pl.ds(offset, 1), :] * pltpu.roll(window, offset, 0)[PAD:]
        half = 0.5 * convolved
        activated = (half + half * jnp.tanh(half)).astype(BF16)
        erased = rows[pl.ds(start + PAD, chunk), :]
        gates = dot_nt(gate[...], activated)
        input_log = 15.0 * jnp.tanh((gates[0:1] + bias_ref[0, 0]) / 15.0)
        forget = gates[1:2] + bias_ref[0, 1]
        forget_log = jnp.minimum(forget, 0.0) - jnp.log1p(jnp.exp(-jnp.abs(forget)))
        summed = jnp.dot(
            jnp.broadcast_to(forget_log, (8, chunk)),
            (line <= lane).astype(F32),
            preferred_element_type=F32,
            precision=lax.Precision.HIGHEST,
        )
        cumulated = summed[0:1]
        last = summed[0:1, chunk - 1 : chunk]
        by_row = as_column(cumulated, line == lane)
        queries = dot_nn(activated, proj[:, :width]).astype(BF16)
        key_rows = (dot_nn(activated, proj[:, width : 2 * width]) * width ** (-0.5)).astype(BF16)
        values = dot_nn(erased, proj[:, 2 * width :]).astype(BF16)
        keys[here, :] = key_rows
        vals[here, :] = values
        exponent = by_row + (input_log - cumulated)
        weights = dot_nt(queries, key_rows) * jnp.exp(jnp.where(line >= lane, exponent, -jnp.inf))
        numerator = dot_nn(weights.astype(BF16), values)

        def earlier(other, total):
            there = pl.ds(other * chunk if small else pl.multiple_of(other * chunk, chunk), chunk)
            tail = tails[other]
            scores = dot_nt(queries, keys[there, :])
            weights = (scores * jnp.exp(by_row + tail[0:1])).astype(BF16)
            tails[other] = tail + last
            return total + dot_nn(weights, vals[there, :])

        numerator = loop(index, earlier, numerator)
        tails[index] = jnp.broadcast_to(last - cumulated + input_log, (8, chunk))
        mean = jnp.mean(numerator, axis=1, keepdims=True)
        centred = numerator - mean
        variance = jnp.mean(centred * centred, axis=1, keepdims=True)
        normed = (centred * lax.rsqrt(variance + 1e-05) * gain[...]).astype(BF16)
        if swap:

            @pl.when(index == 0)
            def _():
                give.wait_recv()

        for side, target in routes:
            product = dot_nn(normed, down[side]).astype(BF16)
            for position in range(GROUP):
                block = index * GROUP + position
                part[side, block] = product[position * tok : (position + 1) * tok]
                mine = (block == seq) & (target == head)

                @pl.when(jnp.logical_not(mine))
                def _():
                    part_copy(side, block, target).start()

                @pl.when(mine)
                def _():
                    pltpu.make_async_copy(
                        part.at[side, block], landed.at[head, side, out_slot], self_sem
                    ).start()

        return carry

    loop(chunks, work, 0)

    for slot in range(per_head):
        for side in range(sides):
            source = lax.rem(head + side, n_head) * per_head + slot
            for other in range(n_head):
                mine = (source == seq) & (other == head)

                @pl.when(jnp.logical_not(mine))
                def _():
                    pltpu.make_async_remote_copy(
                        src_ref=part.at[0, 0],
                        dst_ref=landed.at[other, side, slot],
                        send_sem=part_send.at[0, 0],
                        recv_sem=part_recv.at[other, side, slot],
                        device_id={"seq": sibling},
                        device_id_type=MESH,
                    ).wait_recv()

                @pl.when(mine)
                def _():
                    pltpu.make_async_copy(part.at[0, 0], landed.at[0, 0, 0], self_sem).wait()

            total = landed[0, side, slot].astype(F32)
            for other in range(1, n_head):
                total += landed[other, side, slot].astype(F32)
            place = pl.ds((slot * sides + side) * piece, piece)
            out_ref[0, :, place] = (resid[:, place].astype(F32) + total).astype(BF16)

    def sent_rows(step, carry):
        row_copy(seq, sibling, step).wait_send()
        return carry

    loop(n_seq - 1, sent_rows, 0)
    if swap:
        give.wait_send()

    def sent_parts(block, carry):
        for side, target in routes:

            @pl.when(jnp.logical_not((block == seq) & (target == head)))
            def _():
                part_copy(side, block, target).wait_send()

        return carry

    loop(n_seq, sent_parts, 0)


def body(
    n_seq,
    n_head,
    inner,
    residual_in,
    erase,
    conv_weight,
    qkv_weight,
    gate_weight,
    gate_bias,
    norm_gain,
    down_weight,
):
    tok, width = inner.shape
    columns = down_weight.shape[1]
    tokens = tok * n_seq
    chunk = GROUP * tok
    sides = 2 if n_head == 2 and columns % 256 == 0 else 1
    piece = columns // sides
    per_head = n_seq // n_head
    vmem = pl.BlockSpec(memory_space=pltpu.VMEM)
    anywhere = pl.BlockSpec(memory_space=pl.ANY)
    return pl.pallas_call(
        functools.partial(kernel, n_seq, n_head),
        out_shape=jax.ShapeDtypeStruct((1, tok, residual_in.shape[1]), BF16),
        in_specs=[anywhere] * 4 + [pl.BlockSpec(memory_space=pltpu.SMEM)] + [anywhere] * 4,
        out_specs=vmem,
        scratch_shapes=[
            pltpu.VMEM(inner.shape, BF16),
            pltpu.VMEM(erase.shape, jnp.int32),
            pltpu.VMEM(conv_weight.shape, F32),
            pltpu.VMEM(gate_weight.shape[1:], BF16),
            pltpu.VMEM((1, width), F32),
            pltpu.VMEM(qkv_weight.shape[1:], BF16),
            pltpu.VMEM((sides, width, piece), BF16),
            pltpu.VMEM((width, piece), BF16),
            pltpu.VMEM(residual_in.shape, BF16),
            pltpu.VMEM((PAD + tokens, width), BF16),
            pltpu.VMEM((tokens, width), BF16),
            pltpu.VMEM((tokens, width), BF16),
            pltpu.VMEM((tokens // chunk, 8, chunk), F32),
            pltpu.VMEM((sides, n_seq, tok, piece), BF16),
            pltpu.VMEM((n_head, sides, per_head, tok, piece), BF16),
            pltpu.SemaphoreType.DMA((9,)),
            pltpu.SemaphoreType.DMA((n_seq,)),
            pltpu.SemaphoreType.DMA((n_seq,)),
            pltpu.SemaphoreType.DMA((2,)),
            pltpu.SemaphoreType.DMA((sides, n_seq)),
            pltpu.SemaphoreType.DMA((n_head, sides, per_head)),
            pltpu.SemaphoreType.DMA,
        ],
        compiler_params=pltpu.CompilerParams(
            collective_id=0, has_side_effects=True, vmem_limit_bytes=62 * 2**20
        ),
    )(
        inner,
        erase,
        conv_weight,
        gate_weight,
        gate_bias,
        norm_gain.reshape(1, width),
        qkv_weight,
        down_weight,
        residual_in,
    )


def solution(mesh):
    in_specs = (
        P("seq", "head"),
        P("seq", "head"),
        P("var", "seq"),
        P(None, "head"),
        P("head", None, None),
        P("head", None, None),
        P("head", None),
        P("head"),
        P("head", "seq"),
    )
    out_specs = P("var", "seq", "head")
    run = functools.partial(body, mesh.shape["seq"], mesh.shape["head"])
    return jax.shard_map(run, mesh=mesh, in_specs=in_specs, out_specs=out_specs, check_vma=False)
```

time: 47.6 us -> 31.4 us (0.66); the launches traced: 46.9 us -> 31.2 us
  Pallas kernels: 38.6 us -> 29.5 us
  local copies, waits for them, and re-layouts: 8.31 us -> 1.67 us
    pallas_call x1, Pallas kernels: 38.6 us -> 29.5 us  [body(): pl.pallas_call(functools.partial(kernel, n_seq, n_head), out_shape=jax.Sh...]
    unnamed x19 -> x1, local copies, waits for them, and re-layouts: 8.31 us -> 1.67 us
where the time goes in v2:
time: 31.4 us; the launch traced here: 31.2 us
  Pallas kernels  29.5 us (94%)
  local copies, waits for them, and re-layouts  1.67 us (5%)
    pallas_call x1, Pallas kernels, body(): pl.pallas_call(functools.partial(kernel, n_seq, n_head), out_shape=jax.Sh...  29.5 us
    unnamed x1, local copies, waits for them, and re-layouts  1.67 us

profile of v2, /device:TPU:31, one launch (start us, length us, event | category | flops | bytes accessed | tf_op | source)
XLA Modules:
  0.0 31.2 jit_solution(8458126554563740060)
XLA Ops:
  0.0 29.5 %shard_map.91 = bf16[1,64,2048]{2,1,0:T(8,128)(2,1)} custom-call(bf16[64,512]{1,0:T(8,128)(2,1)} %inner_hbm.1, s32[1,64]{1,0:T(1,128)} %erase_hbm.1, f32[4,512]{1,0:T(4,128)} %conv_hbm.1, bf16[1,2,512]{2,1,0:T(2,128)(2,1)} %gate_hbm.1, f32[1,2]{1,0:T(1,128)} %bias_ref.1, f32[1,512]{1,0:T(1,128)} %bitcast.1, bf16[1,512,1536]{2,1,0:T(8,128)(2,1)} %proj_hbm.1, ...), custom_call_target="tpu_custom_call" | custom-call | tf_op jit(solution)/shard_map/pallas_call | solution.py:337
  29.5 1.7 %copy.11 = bf16[1,64,2048]{2,1,0:T(8,128)(2,1)} copy(bf16[1,64,2048]{2,1,0:T(8,128)(2,1)} %shard_map.91) | data formatting | bytes 524288

commit v3 on v2

--- a/solution.py
+++ b/solution.py
@@ -336,7 +336,7 @@
     anywhere = pl.BlockSpec(memory_space=pl.ANY)
     return pl.pallas_call(
         functools.partial(kernel, n_seq, n_head),
-        out_shape=jax.ShapeDtypeStruct((1, tok, residual_in.shape[1]), BF16),
+        out_shape=pltpu.VMEM((1, tok, residual_in.shape[1]), BF16),
         in_specs=[anywhere] * 4 + [pl.BlockSpec(memory_space=pltpu.SMEM)] + [anywhere] * 4,
         out_specs=vmem,
         scratch_shapes=[

time: 31.4 us -> 29.7 us (0.946)
  local copies, waits for them, and re-layouts: 1.67 us -> 0.71 us
  Pallas kernels: 29.5 us -> 28.8 us
    unnamed x1, local copies, waits for them, and re-layouts: 1.67 us -> 0.71 us
    pallas_call x1, Pallas kernels: 29.5 us -> 28.8 us  [body(): pl.pallas_call(functools.partial(kernel, n_seq, n_head), out_shape=pltpu....]
where the time goes in v3:
time: 29.7 us; the launch traced here: 29.6 us
  Pallas kernels  28.8 us (97%)
  local copies, waits for them, and re-layouts  0.71 us (2%)
    pallas_call x1, Pallas kernels, body(): pl.pallas_call(functools.partial(kernel, n_seq, n_head), out_shape=pltpu....  28.8 us
    unnamed x1, local copies, waits for them, and re-layouts  0.71 us

profile of v3, /device:TPU:31, one launch (start us, length us, event | category | flops | bytes accessed | tf_op | source)
XLA Modules:
  0.0 29.6 jit_solution(16071130520067427032)
XLA Ops:
  0.0 28.8 %shard_map.91 = bf16[1,64,2048]{2,1,0:T(8,128)(2,1)S(1)} custom-call(bf16[64,512]{1,0:T(8,128)(2,1)} %inner_hbm.1, s32[1,64]{1,0:T(1,128)} %erase_hbm.1, f32[4,512]{1,0:T(4,128)} %conv_hbm.1, bf16[1,2,512]{2,1,0:T(2,128)(2,1)} %gate_hbm.1, f32[1,2]{1,0:T(1,128)} %bias_ref.1, f32[1,512]{1,0:T(1,128)} %bitcast.1, bf16[1,512,1536]{2,1,0:T(8,128)(2,1)} %proj_hbm.1, ...), custom_call_target="tpu_custom_call" | custom-call | tf_op jit(solution)/shard_map/pallas_call | solution.py:337
  28.9 0.7 %copy.11 = bf16[1,64,2048]{2,1,0:T(8,128)(2,1)} copy(bf16[1,64,2048]{2,1,0:T(8,128)(2,1)S(1)} %shard_map.91) | data formatting | bytes 524288

commit v4 on v3

--- a/solution.py
+++ b/solution.py
@@ -62,6 +62,7 @@
     part_send,
     part_recv,
     self_sem,
+    ready,
 ):
     seq, head = lax.axis_index("seq"), lax.axis_index("head")
     tok, width = inner.shape
@@ -115,7 +116,14 @@
         )
         return carry
 
-    loop(group - 1, greet, 0)
+    if swap:
+        near = [{"seq": lax.rem(seq + 2 * k, n_seq)} for k in range(1, n_seq // 2)]
+        near += [{"seq": sibling}]
+        across = [{"seq": other, "head": 1 - head} for other in (seq, sibling)]
+        for target in near + across:
+            pl.semaphore_signal(barrier, inc=1, device_id=target, device_id_type=MESH)
+    else:
+        loop(group - 1, greet, 0)
 
     rows[pl.ds(0, PAD), :] = jnp.zeros((PAD, width), BF16)
     line = lax.broadcasted_iota(jnp.int32, (tok, tok), 0)
@@ -128,7 +136,7 @@
     for load in loads[2:]:
         load.wait()
 
-    pl.semaphore_wait(barrier, group - 1)
+    pl.semaphore_wait(barrier, n_seq // 2 + 2 if swap else group - 1)
 
     def row_copy(block, target, slot):
         place = pl.ds(pl.multiple_of(PAD + block * tok, PAD), tok)
@@ -165,6 +173,9 @@
         return carry
 
     loop(n_seq // 2 - 1, forward, 0)
+    if swap:
+        for target in across:
+            pl.semaphore_signal(ready, inc=1, device_id=target, device_id_type=MESH)
 
     line = lax.broadcasted_iota(jnp.int32, (chunk, chunk), 0)
     lane = lax.broadcasted_iota(jnp.int32, (chunk, chunk), 1)
@@ -243,6 +254,7 @@
             @pl.when(index == 0)
             def _():
                 give.wait_recv()
+                pl.semaphore_wait(ready, 2)
 
         for side, target in routes:
             product = dot_nn(normed, down[side]).astype(BF16)
@@ -362,6 +374,7 @@
             pltpu.SemaphoreType.DMA((sides, n_seq)),
             pltpu.SemaphoreType.DMA((n_head, sides, per_head)),
             pltpu.SemaphoreType.DMA,
+            pltpu.SemaphoreType.REGULAR,
         ],
         compiler_params=pltpu.CompilerParams(
             collective_id=0, has_side_effects=True, vmem_limit_bytes=62 * 2**20

time: 29.7 us -> 29.3 us (0.987)
  Pallas kernels: 28.8 us -> 28.4 us
    pallas_call x1, Pallas kernels: 28.8 us -> 28.4 us  [body(): pl.pallas_call(functools.partial(kernel, n_seq, n_head), out_shape=pltpu....]
where the time goes in v4:
time: 29.3 us; the launch traced here: 29.1 us
  Pallas kernels  28.4 us (97%)
  local copies, waits for them, and re-layouts  0.71 us (2%)
    pallas_call x1, Pallas kernels, body(): pl.pallas_call(functools.partial(kernel, n_seq, n_head), out_shape=pltpu....  28.4 us
    unnamed x1, local copies, waits for them, and re-layouts  0.71 us

profile of v4, /device:TPU:31, one launch (start us, length us, event | category | flops | bytes accessed | tf_op | source)
XLA Modules:
  0.0 29.1 jit_solution(15054923855295751921)
XLA Ops:
  0.0 28.4 %shard_map.91 = bf16[1,64,2048]{2,1,0:T(8,128)(2,1)S(1)} custom-call(bf16[64,512]{1,0:T(8,128)(2,1)} %inner_hbm.1, s32[1,64]{1,0:T(1,128)} %erase_hbm.1, f32[4,512]{1,0:T(4,128)} %conv_hbm.1, bf16[1,2,512]{2,1,0:T(2,128)(2,1)} %gate_hbm.1, f32[1,2]{1,0:T(1,128)} %bias_ref.1, f32[1,512]{1,0:T(1,128)} %bitcast.1, bf16[1,512,1536]{2,1,0:T(8,128)(2,1)} %proj_hbm.1, ...), custom_call_target="tpu_custom_call" | custom-call | tf_op jit(solution)/shard_map/pallas_call | solution.py:349
  28.4 0.7 %copy.11 = bf16[1,64,2048]{2,1,0:T(8,128)(2,1)} copy(bf16[1,64,2048]{2,1,0:T(8,128)(2,1)S(1)} %shard_map.91) | data formatting | bytes 524288

commit v5 on v4

--- a/solution.py
+++ b/solution.py
@@ -83,6 +83,29 @@
             return carry
         return lax.fori_loop(0, count, step, carry)
 
+    barrier = pltpu.get_barrier_semaphore()
+    group = n_seq * n_head
+    flat = seq * n_head + head
+
+    def greet(step, carry):
+        other = lax.rem(flat + step + 1, group)
+        pl.semaphore_signal(
+            barrier,
+            inc=1,
+            device_id={"seq": other // n_head, "head": lax.rem(other, n_head)},
+            device_id_type=MESH,
+        )
+        return carry
+
+    if swap:
+        near = [{"seq": lax.rem(seq + 2 * k, n_seq)} for k in range(1, n_seq // 2)]
+        near += [{"seq": sibling}]
+        across = [{"seq": other, "head": 1 - head} for other in (seq, sibling)]
+        for target in near + across:
+            pl.semaphore_signal(barrier, inc=1, device_id=target, device_id_type=MESH)
+    else:
+        loop(group - 1, greet, 0)
+
     loads = [
         pltpu.make_async_copy(source, target, load_sem.at[index])
         for index, (source, target) in enumerate(
@@ -102,29 +125,6 @@
     for load in loads:
         load.start()
 
-    barrier = pltpu.get_barrier_semaphore()
-    group = n_seq * n_head
-    flat = seq * n_head + head
-
-    def greet(step, carry):
-        other = lax.rem(flat + step + 1, group)
-        pl.semaphore_signal(
-            barrier,
-            inc=1,
-            device_id={"seq": other // n_head, "head": lax.rem(other, n_head)},
-            device_id_type=MESH,
-        )
-        return carry
-
-    if swap:
-        near = [{"seq": lax.rem(seq + 2 * k, n_seq)} for k in range(1, n_seq // 2)]
-        near += [{"seq": sibling}]
-        across = [{"seq": other, "head": 1 - head} for other in (seq, sibling)]
-        for target in near + across:
-            pl.semaphore_signal(barrier, inc=1, device_id=target, device_id_type=MESH)
-    else:
-        loop(group - 1, greet, 0)
-
     rows[pl.ds(0, PAD), :] = jnp.zeros((PAD, width), BF16)
     line = lax.broadcasted_iota(jnp.int32, (tok, tok), 0)
     lane = lax.broadcasted_iota(jnp.int32, (tok, tok), 1)
@@ -133,9 +133,6 @@
     kept = as_column((1 - erase[...]).astype(F32), line == lane)
     own = pl.ds(pl.multiple_of(PAD + seq * tok, PAD), tok)
     rows[own, :] = (inner[...].astype(F32) * kept).astype(BF16)
-    for load in loads[2:]:
-        load.wait()
-
     pl.semaphore_wait(barrier, n_seq // 2 + 2 if swap else group - 1)
 
     def row_copy(block, target, slot):
@@ -163,6 +160,7 @@
         device_id={"seq": partner},
         device_id_type=MESH,
     )
+    loads[2].wait()
     if swap:
         give.start()
 
@@ -177,6 +175,8 @@
         for target in across:
             pl.semaphore_signal(ready, inc=1, device_id=target, device_id_type=MESH)
 
+    for load in loads[3:]:
+        load.wait()
     line = lax.broadcasted_iota(jnp.int32, (chunk, chunk), 0)
     lane = lax.broadcasted_iota(jnp.int32, (chunk, chunk), 1)
 

time: 29.3 us -> 29.2 us (level)
  no operation moved by 1% of the time
where the time goes in v5:
time: 29.2 us; the launch traced here: 29.1 us
  Pallas kernels  28.4 us (97%)
  local copies, waits for them, and re-layouts  0.71 us (2%)
    pallas_call x1, Pallas kernels, body(): pl.pallas_call(functools.partial(kernel, n_seq, n_head), out_shape=pltpu....  28.4 us
    unnamed x1, local copies, waits for them, and re-layouts  0.71 us

profile of v5, /device:TPU:31, one launch (start us, length us, event | category | flops | bytes accessed | tf_op | source)
XLA Modules:
  0.0 29.1 jit_solution(17381132234040671839)
XLA Ops:
  0.0 28.4 %shard_map.91 = bf16[1,64,2048]{2,1,0:T(8,128)(2,1)S(1)} custom-call(bf16[64,512]{1,0:T(8,128)(2,1)} %inner_hbm.1, s32[1,64]{1,0:T(1,128)} %erase_hbm.1, f32[4,512]{1,0:T(4,128)} %conv_hbm.1, bf16[1,2,512]{2,1,0:T(2,128)(2,1)} %gate_hbm.1, f32[1,2]{1,0:T(1,128)} %bias_ref.1, f32[1,512]{1,0:T(1,128)} %bitcast.1, bf16[1,512,1536]{2,1,0:T(8,128)(2,1)} %proj_hbm.1, ...), custom_call_target="tpu_custom_call" | custom-call | tf_op jit(solution)/shard_map/pallas_call | solution.py:349
  28.4 0.7 %copy.11 = bf16[1,64,2048]{2,1,0:T(8,128)(2,1)} copy(bf16[1,64,2048]{2,1,0:T(8,128)(2,1)S(1)} %shard_map.91) | data formatting | bytes 524288
